TPU v7x, 32 devices: a whole 2x2x4 slice. The times are simulated.
32 devices in a mesh: grp: 2 (over y), rows: 8 (over z, x), heads: 2 (over core).
Axes of the slice: x: 2, y: 2, z: 4, core: 2. Of those that a mesh axis runs over, the one named last changes fastest.
Arguments:
- pre_state: bfloat16 [32, 128, 64, 128], P(('grp', 'rows'), 'heads'), parts along dimension 0, may hold values from -6 to 6
- pre_conv: bfloat16 [32, 3, 4, 2304], P(('grp', 'rows'), None, 'heads'), parts along dimension 0, may hold values from -6 to 6
- resident_state: bfloat16 [64, 128, 64, 128], P(('grp', 'rows'), 'heads'), parts along dimension 0, may hold values from -6 to 6
- resident_conv: bfloat16 [64, 3, 4, 2304], P(('grp', 'rows'), None, 'heads'), parts along dimension 0, may hold values from -6 to 6
- source_slot: int32 [16], P(('grp', 'rows')), parts along dimension 0, may hold values from 0 to 15, as said below
- target_row: int32 [16], P(('grp', 'rows')), parts along dimension 0, may hold values from 0 to 31, as said below
- conv_input: bfloat16 [4, 64, 4, 2304], P(None, ('grp', 'rows'), 'heads'), parts along dimension 1, may hold values from -6 to 6
- delta_raw: bfloat16 [4, 64, 128], P(None, ('grp', 'rows'), 'heads'), parts along dimension 1, may hold values from -4 to 4
- gate_input: bfloat16 [4, 64, 8192], P(None, ('grp', 'rows'), 'heads'), parts along dimension 1, may hold values from -6 to 6
- active: int32 [4, 64], P(None, ('grp', 'rows')), parts along dimension 1, may hold values 0 or 1
- conv_weight: float32 [4, 4, 2304], P(None, 'heads'), may hold values from -3 to 3
- conv_bias: float32 [4, 2304], P('heads'), may hold values from -0.5 to 0.5
- delta_bias: float32 [128], P('heads'), may hold values from -2 to 0.5
- decay_log: float32 [128], P('heads'), may hold values from -4 to 0.5
- skip_gain: float32 [128], P('heads'), may hold values from 0.5 to 2
- norm_gain: float32 [8192], P('heads'), may hold values from 0.5 to 1.5
Outputs:
- layer_output: bfloat16 [4, 64, 8192], P(None, ('grp', 'rows'), 'heads'), parts along dimension 1
- final_state: bfloat16 [64, 128, 64, 128], P(('grp', 'rows'), 'heads'), parts along dimension 0
- final_conv: bfloat16 [64, 3, 4, 2304], P(('grp', 'rows'), None, 'heads'), parts along dimension 0
There are 2 independent parts, one for each index of `grp`. A program takes and returns all parts, laid end to end along the dimension named above; an argument that names none is the same for every part. Nothing has to cross between parts.
Inputs may be any that keep to these rules, and one draw needn't show every extreme that they name: `source_slot`: 8 distinct slots. `target_row`: 8 distinct rows; the 4 rows of one index of rows receive at most 4 prompts, and in every draw some index receives 4.
All inputs are finite; a program needn't handle non-finite values. No bound on the sum of `active` on one device may be relied on, other than what follows from the above.
Results may differ from a plain program's by a relative error of at most 0.001.
Values may be sent and summed in bfloat16 or wider, within the bound.
A program may use at most 64 MiB of HBM per device.

v0:
```python
import jax
import jax.numpy as jnp
from jax import lax
from jax.sharding import PartitionSpec as P


def decode_block(
    states,
    conv_rows,
    conv_input,
    delta_raw,
    gate_input,
    active,
    conv_weight,
    conv_bias,
    delta_bias,
    decay_log,
    skip_gain,
    norm_gain,
):
    steps_total = conv_input.shape[0]
    row_count, head_count, head_size, state_size = states.shape
    group_count = conv_rows.shape[2]
    per_group = head_count // group_count
    value_width = per_group * head_size
    carried = states.astype(jnp.float32)
    history = conv_rows.astype(jnp.float32)
    decay_rates = jnp.exp(decay_log)
    results = []
    for step_index in range(steps_total):
        window = jnp.concatenate(
            [history, conv_input[step_index][:, None].astype(jnp.float32)], axis=1
        )
        convolved = jax.nn.silu(jnp.sum(window * conv_weight[None], axis=1) + conv_bias[None])
        inputs = convolved[..., :value_width].reshape(row_count, head_count, head_size)
        write_heads = jnp.repeat(
            convolved[..., value_width : value_width + state_size], per_group, axis=1
        )
        read_heads = jnp.repeat(convolved[..., value_width + state_size :], per_group, axis=1)
        step_size = jax.nn.softplus(delta_raw[step_index].astype(jnp.float32) + delta_bias[None])
        retention = jnp.exp(-decay_rates[None] * step_size)
        updated = (
            retention[:, :, None, None] * carried
            + (step_size[:, :, None] * inputs)[..., None] * write_heads[:, :, None, :]
        )
        readout = (
            jnp.sum(updated * read_heads[:, :, None, :], axis=-1)
            + skip_gain[None, :, None] * inputs
        )
        gated_out = readout.reshape(row_count, head_count * head_size) * jax.nn.silu(
            gate_input[step_index].astype(jnp.float32)
        )
        grouped = gated_out.reshape(row_count, group_count, value_width)
        inverse_rms = lax.rsqrt(jnp.mean(grouped * grouped, axis=-1, keepdims=True) + 1e-05)
        normed = (grouped * inverse_rms).reshape(row_count, head_count * head_size) * norm_gain[
            None
        ]
        live_rows = active[step_index] == 1
        carried = jnp.where(live_rows[:, None, None, None], updated, carried)
        history = jnp.where(live_rows[:, None, None, None], window[:, 1:], history)
        results.append(
            jnp.where(live_rows[:, None], normed, jnp.zeros_like(normed)).astype(jnp.bfloat16)
        )
    return (jnp.stack(results), carried.astype(jnp.bfloat16), history.astype(jnp.bfloat16))


def route_pieces(received, slot_for_row, halves, slot_count, row_devices, rows_here):
    flattened = received.reshape(-1, received.shape[-1])
    slot_rows = slot_for_row.reshape(row_devices, 1, rows_here)
    half_index = jnp.arange(halves, dtype=jnp.int32)[None, :, None]
    positions = (
        slot_rows // slot_count * (halves * slot_count)
        + half_index * slot_count
        + slot_rows % slot_count
    )
    picked = flattened[positions.reshape(-1)]
    return picked.reshape(row_devices * halves, rows_here, 1, received.shape[-1])


def per_device(
    pre_state,
    pre_conv,
    resident_state,
    resident_conv,
    source_slot,
    target_row,
    conv_input,
    delta_raw,
    gate_input,
    active,
    conv_weight,
    conv_bias,
    delta_bias,
    decay_log,
    skip_gain,
    norm_gain,
):
    all_source, all_target = (
        lax.all_gather(source_slot, "rows", axis=0, tiled=True),
        lax.all_gather(target_row, "rows", axis=0, tiled=True),
    )
    row_devices = lax.axis_size("rows")
    rows_here = resident_state.shape[0]
    slot_count = pre_state.shape[0]
    total_rows = row_devices * rows_here
    matches = all_target[None, :] == jnp.arange(total_rows, dtype=jnp.int32)[:, None]
    arrival = jnp.any(matches, axis=1)
    slot_for_row = jnp.sum(jnp.where(matches, all_source[None, :], 0), axis=1)
    own_arrival = lax.dynamic_slice_in_dim(arrival, lax.axis_index("rows") * rows_here, rows_here)
    halves = 1
    state_pieces = pre_state.reshape(slot_count, row_devices, -1)
    conv_pieces = pre_conv.reshape(slot_count, row_devices, -1)
    piece_state, piece_conv = (
        lax.all_to_all(state_pieces, "rows", split_axis=1, concat_axis=0, tiled=True),
        lax.all_to_all(conv_pieces, "rows", split_axis=1, concat_axis=0, tiled=True),
    )
    outgoing_state = route_pieces(
        piece_state, slot_for_row, halves, slot_count, row_devices, rows_here
    )
    outgoing_conv = route_pieces(
        piece_conv, slot_for_row, halves, slot_count, row_devices, rows_here
    )
    came_state, came_conv = (
        lax.all_to_all(outgoing_state, "rows", split_axis=0, concat_axis=2, tiled=True),
        lax.all_to_all(outgoing_conv, "rows", split_axis=0, concat_axis=2, tiled=True),
    )
    arrived_state = came_state.reshape(resident_state.shape)
    arrived_conv = came_conv.reshape(resident_conv.shape)
    row_flags = own_arrival[:, None, None, None]
    start_state = jnp.where(row_flags, arrived_state, resident_state)
    start_conv = jnp.where(row_flags, arrived_conv, resident_conv)
    return decode_block(
        start_state,
        start_conv,
        conv_input,
        delta_raw,
        gate_input,
        active,
        conv_weight,
        conv_bias,
        delta_bias,
        decay_log,
        skip_gain,
        norm_gain,
    )


def solution(mesh):
    in_specs = (
        P(("grp", "rows"), "heads", None, None),
        P(("grp", "rows"), None, "heads", None),
        P(("grp", "rows"), "heads", None, None),
        P(("grp", "rows"), None, "heads", None),
        P(("grp", "rows")),
        P(("grp", "rows")),
        P(None, ("grp", "rows"), "heads", None),
        P(None, ("grp", "rows"), "heads"),
        P(None, ("grp", "rows"), "heads"),
        P(None, ("grp", "rows")),
        P(None, "heads", None),
        P("heads", None),
        P("heads"),
        P("heads"),
        P("heads"),
        P("heads"),
    )
    out_specs = (
        P(None, ("grp", "rows"), "heads"),
        P(("grp", "rows"), "heads", None, None),
        P(("grp", "rows"), None, "heads", None),
    )
    return jax.shard_map(
        per_device, mesh=mesh, in_specs=in_specs, out_specs=out_specs, check_vma=False
    )
```

profile of v0, /device:TPU:0, one launch (start us, length us, event | category | flops | bytes accessed | tf_op | source)
XLA Modules:
  0.0 243.4 jit_solution(12745731516262506721)
XLA Ops:
  0.6 0.9 reshape.882
  1.6 0.7 copy.36
  2.2 7.3 %all-to-all-start.2 = ((bf16[2,8,1728]{2,0,1:T(2,128)(2,1)}), bf16[2,8,1728]{2,0,1:T(2,128)(2,1)S(1)}, u32[]{:S(2)}, u32[]{:S(2)}) async-start(bf16[2,8,1728]{2,0,1:T(2,128)(2,1)} %copy.36), calls=%async_computation.2 | async-start | bytes 114688 | tf_op jit(solution)/shard_map/all_to_all | solution.py:115
  9.5 2.1 reshape.878
  11.7 3.5 %copy.33 = bf16[2,8,65536]{2,0,1:T(2,128)(2,1)} copy(bf16[2,8,65536]{2,1,0:T(8,128)(2,1)S(1)} %reshape.878) | data formatting | bytes 4194304 | tf_op jit(solution)/shard_map/reshape | solution.py:111
  15.1 1.2 all-to-all-done.2
  16.3 4.8 %all-to-all-start = ((bf16[2,8,65536]{2,0,1:T(2,128)(2,1)}), bf16[2,8,65536]{2,0,1:T(2,128)(2,1)S(1)}, u32[]{:S(2)}, u32[]{:S(2)}) async-start(bf16[2,8,65536]{2,0,1:T(2,128)(2,1)} %copy.33), calls=%async_computation | async-start | bytes 4194304 | tf_op jit(solution)/shard_map/all_to_all | solution.py:114
  22.4 0.6 dynamic-slice
  23.0 0.8 dynamic-update-slice
  23.8 0.8 dynamic-update-slice.1
  24.5 44.5 %all-reduce.2 = (s32[8]{0:T(128)S(1)}, s32[8]{0:T(128)S(1)}) all-reduce(s32[8]{0:T(128)S(1)} %dynamic-update-slice.1, s32[8]{0:T(128)S(1)} %dynamic-update-slice), channel_id=1, replica_groups=mesh['grp'=2,'rows'=8,'heads'=2] {'rows'}, use_global_device_ids=true, to_apply=%add.1 | all-reduce | flops 16 | bytes 128
  69.2 0.6 gather_fusion.1
  69.8 0.7 reshape.884
  70.5 3.6 %all-to-all-start.3 = ((bf16[8,4,1,1728]{3,1,2,0:T(4,128)(2,1)}), bf16[8,4,1,1728]{3,1,2,0:T(4,128)(2,1)S(1)}, u32[]{:S(2)}, u32[]{:S(2)}) async-start(bf16[8,4,1,1728]{3,1,2,0:T(4,128)(2,1)} %bitcast.12), calls=%async_computation.3 | async-start | bytes 229376 | tf_op jit(solution)/shard_map/all_to_all | solution.py:125
  74.1 2.1 reshape.879
  76.2 5.3 %gather_fusion = bf16[32,65536]{1,0:T(8,128)(2,1)} fusion(bf16[16,65536]{1,0:T(8,128)(2,1)S(1)} %reshape.879, s32[1024]{0:T(1024)S(1)} %pad_clamp_fusion), kind=kCustom, calls=%fused_computation | custom fusion | bytes 8388736 | tf_op jit(solution)/shard_map/gather | solution.py:76
  81.6 5.3 %reshape.880 = bf16[8,4,1,65536]{3,1,0,2:T(4,128)(2,1)} reshape(bf16[32,65536]{1,0:T(8,128)(2,1)} %gather_fusion) | data formatting | bytes 8388608 | tf_op jit(solution)/shard_map/reshape | solution.py:77
  87.0 6.1 %all-to-all-start.1 = ((bf16[8,4,1,65536]{3,1,2,0:T(4,128)(2,1)}), bf16[8,4,1,65536]{3,1,2,0:T(4,128)(2,1)}, u32[]{:S(2)}, u32[]{:S(2)}) async-start(bf16[8,4,1,65536]{3,1,2,0:T(4,128)(2,1)} %bitcast.90), calls=%async_computation.1 | async-start | bytes 8388608 | tf_op jit(solution)/shard_map/all_to_all | solution.py:124
  94.1 0.2 reshape.885
  94.7 0.2 fusion.16
  95.1 0.7 fusion.7
  95.8 0.3 divide_multiply_fusion.3
  97.1 0.8 fusion.19
  97.9 88.1 %all-to-all-done.1 = bf16[8,4,1,65536]{3,1,2,0:T(4,128)(2,1)} async-done(((bf16[8,4,1,65536]{3,1,2,0:T(4,128)(2,1)}), bf16[8,4,1,65536]{3,1,2,0:T(4,128)(2,1)}, u32[]{:S(2)}, u32[]{:S(2)}) %all-to-all-start.1) | async-done | bytes 4194336 | tf_op jit(solution)/shard_map/all_to_all | solution.py:124
  186.0 6.5 %copy.35 = bf16[1,4,8,1,65536]{4,2,1,3,0:T(8,128)(2,1)} copy(bf16[1,4,8,1,65536]{4,1,2,3,0:T(4,128)(2,1)} %bitcast.9) | data formatting | bytes 8388608 | tf_op jit(solution)/shard_map/all_to_all | solution.py:124
  192.5 5.6 %reshape.881 = bf16[4,64,64,128]{3,2,1,0:T(8,128)(2,1)} reshape(bf16[1,4,8,1,65536]{4,2,1,3,0:T(8,128)(2,1)} %copy.35) | data formatting | bytes 8388608 | tf_op jit(solution)/shard_map/reshape | solution.py:127
  198.2 14.9 %select_convert_fusion = (bf16[4,64,64,128]{3,2,1,0:T(8,128)(2,1)}, bf16[4,64,64,128]{3,2,1,0:T(8,128)(2,1)S(1)}) fusion(f32[4,64,128]{2,1,0:T(8,128)S(1)} %bitcast.99, f32[4,64,64]{2,1,0:T(8,128)S(1)} %get-tuple-element.74, f32[4,64]{1,0:T(4,128)S(1)} %get-tuple-element.64, f32[4,64,128]{2,1,0:T(8,128)S(1)} %bitcast.97, ...), kind=kLoop, calls=%fused_computation.5 | loop fusion | flops 39845888 | bytes 17567764 | tf_op jit(solution)/shard_map/convert_element_type | solution.py:64
  213.2 1.9 copy-done
  215.1 18.7 %multiply_reduce_fusion.1 = (f32[4,64,64]{2,1,0:T(8,128)S(1)}, f32[4,64,64]{2,1,0:T(8,128)S(1)}, f32[4,64,64]{2,1,0:T(8,128)S(1)}) fusion(bf16[4,64,64,128]{3,2,1,0:T(8,128)(2,1)S(1)} %get-tuple-element.13, f32[4,64,128]{2,1,0:T(8,128)S(1)} %bitcast.103, f32[4,64,128]{2,1,0:T(8,128)S(1)} %bitcast.98, f32[4,64,64]{2,1,0:T(8,128)S(1)} %get-tuple-element.75, ...), kind=kLoop, calls=%fused_computation.8 | loop fusion | flops 46088192 | bytes 5574668 | tf_op jit(solution)/shard_map/reduce_sum | solution.py:47
  234.2 7.0 %multiply_reduce_fusion.3 = f32[4,64,64]{2,1,0:T(8,128)S(1)} fusion(bf16[4,64,64,128]{3,2,1,0:T(8,128)(2,1)} %copy-done, f32[4,64,128]{2,1,0:T(8,128)S(1)} %bitcast.101, f32[4,64,128]{2,1,0:T(8,128)S(1)} %bitcast.94, f32[4,64,64]{2,1,0:T(8,128)S(1)} %get-tuple-element.77, f32[4,64]{1,0:T(4,128)S(1)} %get-tuple-element.24), kind=kLoop, calls=%fused_computation.14 | loop fusion | flops 12566528 | bytes 4588544 | tf_op jit(solution)/shard_map/reduce_sum | solution.py:47
  241.2 0.5 multiply_reduce_fusion.7
  242.6 0.8 pad_maximum_fusion.4
  (90 shorter events, 3.8 us)
Async XLA Ops:
  2.2 14.1 %all-to-all-start.2 = ((bf16[2,8,1728]{2,0,1:T(2,128)(2,1)}), bf16[2,8,1728]{2,0,1:T(2,128)(2,1)S(1)}, u32[]{:S(2)}, u32[]{:S(2)}) async-start(bf16[2,8,1728]{2,0,1:T(2,128)(2,1)} %copy.36), calls=%async_computation.2 | async-start | bytes 114688 | tf_op jit(solution)/shard_map/all_to_all | solution.py:115
  11.6 10.8 %copy-start.13 = (u32[32]{0:T(128)S(1)}, u32[32]{0:T(128)}, u32[]{:S(2)}) copy-start(u32[32]{0:T(128)} %constant.88) | copy-start | bytes 388
  16.3 54.1 %all-to-all-start = ((bf16[2,8,65536]{2,0,1:T(2,128)(2,1)}), bf16[2,8,65536]{2,0,1:T(2,128)(2,1)S(1)}, u32[]{:S(2)}, u32[]{:S(2)}) async-start(bf16[2,8,65536]{2,0,1:T(2,128)(2,1)} %copy.33), calls=%async_computation | async-start | bytes 4194304 | tf_op jit(solution)/shard_map/all_to_all | solution.py:114
  70.5 3.6 %copy-start.1 = (bf16[2,8,65536]{2,0,1:T(2,128)(2,1)}, bf16[2,8,65536]{2,0,1:T(2,128)(2,1)S(1)}, u32[]{:S(2)}) copy-start(bf16[2,8,65536]{2,0,1:T(2,128)(2,1)S(1)} %all-to-all-done) | copy-start | bytes 6291460
  70.5 16.4 %all-to-all-start.3 = ((bf16[8,4,1,1728]{3,1,2,0:T(4,128)(2,1)}), bf16[8,4,1,1728]{3,1,2,0:T(4,128)(2,1)S(1)}, u32[]{:S(2)}, u32[]{:S(2)}) async-start(bf16[8,4,1,1728]{3,1,2,0:T(4,128)(2,1)} %bitcast.12), calls=%async_computation.3 | async-start | bytes 229376 | tf_op jit(solution)/shard_map/all_to_all | solution.py:125
  86.9 6.2 %copy-start.3 = (bf16[4,4,4096]{2,1,0:T(4,128)(2,1)S(1)}, bf16[4,4,4096]{2,1,0:T(4,128)(2,1)}, u32[]{:S(2)}) copy-start(bf16[4,4,4096]{2,1,0:T(4,128)(2,1)} %param.24) | copy-start | bytes 393220
  86.9 6.6 %copy-start.11 = (f32[64]{0:T(128)S(1)}, f32[64]{0:T(128)}, u32[]{:S(2)}) copy-start(f32[64]{0:T(128)} %param.30) | copy-start | bytes 772
  86.9 7.0 %copy-start.12 = (f32[64]{0:T(128)S(1)}, f32[64]{0:T(128)}, u32[]{:S(2)}) copy-start(f32[64]{0:T(128)} %param.29) | copy-start | bytes 772
  86.9 7.0 %copy-start.9 = (s32[4,4]{1,0:T(4,128)S(1)}, s32[4,4]{1,0:T(4,128)}, u32[]{:S(2)}) copy-start(s32[4,4]{1,0:T(4,128)} %param.25) | copy-start | bytes 196
  86.9 7.0 %copy-start.8 = (bf16[4,4,64]{2,1,0:T(4,128)(2,1)S(1)}, bf16[4,4,64]{2,1,0:T(4,128)(2,1)}, u32[]{:S(2)}) copy-start(bf16[4,4,64]{2,1,0:T(4,128)(2,1)} %param.23) | copy-start | bytes 6148
  86.9 7.0 %copy-start.10 = (f32[64]{0:T(128)S(1)}, f32[64]{0:T(128)}, u32[]{:S(2)}) copy-start(f32[64]{0:T(128)} %param.28) | copy-start | bytes 772
  86.9 7.0 %copy-start.2 = (bf16[4,4,2,2304]{3,2,1,0:T(2,128)(2,1)S(1)}, bf16[4,4,2,2304]{3,2,1,0:T(2,128)(2,1)}, u32[]{:S(2)}) copy-start(bf16[4,4,2,2304]{3,2,1,0:T(2,128)(2,1)} %param.22) | copy-start | bytes 442372
  87.0 7.4 %copy-start.4 = (bf16[4,3,2,2304]{3,2,1,0:T(2,128)(2,1)S(1)}, bf16[4,3,2,2304]{3,2,1,0:T(2,128)(2,1)}, u32[]{:S(2)}) copy-start(bf16[4,3,2,2304]{3,2,1,0:T(2,128)(2,1)} %param.19) | copy-start | bytes 331780
  87.0 8.1 %copy-start.5 = (f32[4,2,2304]{2,1,0:T(2,128)S(1)}, f32[4,2,2304]{2,1,0:T(2,128)}, u32[]{:S(2)}) copy-start(f32[4,2,2304]{2,1,0:T(2,128)} %param.26) | copy-start | bytes 221188
  87.0 99.0 %all-to-all-start.1 = ((bf16[8,4,1,65536]{3,1,2,0:T(4,128)(2,1)}), bf16[8,4,1,65536]{3,1,2,0:T(4,128)(2,1)}, u32[]{:S(2)}, u32[]{:S(2)}) async-start(bf16[8,4,1,65536]{3,1,2,0:T(4,128)(2,1)} %bitcast.90), calls=%async_computation.1 | async-start | bytes 8388608 | tf_op jit(solution)/shard_map/all_to_all | solution.py:124
  93.1 2.7 %copy-start.6 = (f32[2,2304]{1,0:T(2,128)S(1)}, f32[2,2304]{1,0:T(2,128)}, u32[]{:S(2)}) copy-start(f32[2,2304]{1,0:T(2,128)} %param.27) | copy-start | bytes 55300
  213.1 1.9 copy-start
  233.8 8.7 %copy-start.7 = (f32[4096]{0:T(1024)S(1)}, f32[4096]{0:T(1024)}, u32[]{:S(2)}) copy-start(f32[4096]{0:T(1024)} %param.31) | copy-start | bytes 49156
where the time goes:
time: 244 us; the launch traced here: 243 us
  waiting for transfers between devices  89.4 us (37%)
  other arithmetic  45.6 us (19%)
  blocking collectives  44.5 us (18%)
  local copies, waits for them, and re-layouts  39.7 us (16%)
  starting transfers between devices  21.8 us (9%)
    all_to_all x1, waiting for transfers between devices, per_device(): lax.all_to_all(outgoing_state, 'rows', split_axis=0, concat_axis=2, tiled...  88.1 us
    unnamed x1, blocking collectives  44.5 us
    reduce_sum x2, other arithmetic, decode_block(): jnp.sum(updated * read_heads[:, :, None, :], axis=-1)  25.7 us
    convert_element_type x1, other arithmetic, decode_block(): carried.astype(jnp.bfloat16)  14.9 us
    all_to_all x1, starting transfers between devices, per_device(): lax.all_to_all(conv_pieces, 'rows', split_axis=1, concat_axis=0, tiled=True)  7.25 us
    all_to_all x1, local copies, waits for them, and re-layouts, per_device(): lax.all_to_all(outgoing_state, 'rows', split_axis=0, concat_axis=2, tiled...  6.5 us
    all_to_all x1, starting transfers between devices, per_device(): lax.all_to_all(outgoing_state, 'rows', split_axis=0, concat_axis=2, tiled...  6.13 us
    reshape x2, local copies, waits for them, and re-layouts, route_pieces(): picked.reshape(row_devices * halves, rows_here, 1, received.shape[-1])  6.01 us
  transfers between devices with their start and end apart: 4, of which 2 were waited for; matrix products, arithmetic and copies ran while one was open for 11% of the time, Pallas kernels for 0%

commit v1 on v0

v1 whole, which is shorter than its diff:
```python
import functools

import jax
import jax.numpy as jnp
from jax import lax
from jax.experimental import pallas as pl
from jax.experimental.pallas import tpu as pltpu
from jax.sharding import PartitionSpec as P

F32 = jnp.float32
BF16 = jnp.bfloat16


def split_two(values):
    high = lax.reduce_precision(values, exponent_bits=8, mantissa_bits=7)
    return high.astype(BF16), (values - high).astype(BF16)


def prepare(
    history,
    conv_input,
    delta_raw,
    gate_input,
    active,
    conv_weight,
    conv_bias,
    delta_bias,
    decay_log,
    skip_gain,
    norm_gain,
    state_size,
    head_size,
):
    steps, rows = conv_input.shape[:2]
    groups = conv_bias.shape[0]
    heads = delta_bias.shape[0]
    per_group = heads // groups
    width = per_group * head_size
    live = active == 1
    history = [history[:, k].astype(F32) for k in range(history.shape[1])]
    decay_rates = jnp.exp(decay_log)
    xs, bs, cs, log_as, deltas = [], [], [], [], []
    for t in range(steps):
        window = history + [conv_input[t].astype(F32)]
        total = window[0] * conv_weight[0][None]
        for k in range(1, len(window)):
            total = total + window[k] * conv_weight[k][None]
        u = jax.nn.silu(total + conv_bias[None])
        xs.append(u[..., :width].reshape(rows, heads, head_size))
        bs.append(u[..., width : width + state_size])
        cs.append(u[..., width + state_size :])
        delta = jax.nn.softplus(delta_raw[t].astype(F32) + delta_bias[None])
        deltas.append(delta)
        log_as.append(-decay_rates[None] * delta)
        keep = live[t][:, None, None]
        history = [jnp.where(keep, window[k + 1], history[k]) for k in range(len(history))]
    final_conv = jnp.stack(history, axis=1).astype(BF16)
    x = jnp.stack(xs, axis=1)
    b = jnp.stack(bs, axis=1)
    c = jnp.stack(cs, axis=1)
    delta = jnp.stack(deltas, axis=1)
    log_a = jnp.stack(log_as, axis=1)
    live_rt = live.T[:, :, None]
    live_log = jnp.where(live_rt, log_a, 0.0)
    live_delta = jnp.where(live_rt, delta, 0.0)
    bc = jnp.sum(b[:, None] * c[:, :, None], axis=-1)
    bc = jnp.repeat(bc, per_group, axis=-1)
    intra, through = [], []
    for t in range(steps):
        part = (skip_gain[None] + delta[:, t] * bc[:, t, t])[..., None] * x[:, t]
        reach = log_a[:, t]
        for s in range(t - 1, -1, -1):
            weight = jnp.exp(reach) * live_delta[:, s] * bc[:, t, s]
            part = part + weight[..., None] * x[:, s]
            reach = reach + live_log[:, s]
        intra.append(part)
        through.append(jnp.exp(reach))
    gate = jax.nn.silu(gate_input.astype(F32)).swapaxes(0, 1)
    y0 = jnp.stack(intra, axis=1).reshape(gate.shape) * gate
    scale = jnp.repeat(jnp.stack(through, axis=1), head_size, axis=-1) * gate
    tails = []
    reach = jnp.zeros_like(live_log[:, 0])
    for s in range(steps - 1, -1, -1):
        tails.append(jnp.exp(reach) * live_delta[:, s])
        reach = reach + live_log[:, s]
    tail = jnp.stack(tails[::-1], axis=1)
    keep_all = jnp.broadcast_to(jnp.exp(reach)[..., None], (rows, heads, state_size))
    coef = (tail[..., None] * x).reshape(rows, steps, heads * head_size)
    coef_hi, coef_lo = split_two(coef)
    b_hi, b_lo = split_two(b.swapaxes(1, 2))
    c_hi, c_lo = split_two(c.swapaxes(1, 2))
    left = jnp.concatenate([coef_hi, coef_hi, coef_lo, jnp.zeros_like(coef_hi)], axis=1)
    right = jnp.concatenate([b_hi, b_lo, b_hi, jnp.zeros_like(b_hi)], axis=2)
    reads = jnp.concatenate([c_hi, c_lo, jnp.zeros_like(c_hi), jnp.zeros_like(c_lo)], axis=2)
    gain = jnp.where(live.T[:, :, None], norm_gain[None, None], 0.0)
    return final_conv, scale, y0, gain, keep_all, left, right, reads


def update_kernel(
    steps, flags, came, resident, scale, y0, gain, keep, left, right, reads, out, final, rows_out
):
    r = pl.program_id(0)
    g = pl.program_id(1)
    per_group, head_size, state_size = resident.shape[1:]
    width = per_group * head_size
    arrived = flags[r] == 1

    def run(source):
        s0 = source.reshape(width, state_size)
        read = lax.dot_general(
            reads[0, 0], s0, (((1,), (1,)), ((), ())), preferred_element_type=F32
        )
        q = read[:steps] + read[steps : 2 * steps]
        v = scale[0] * q + y0[0]
        mean = jnp.mean(v * v, axis=-1, keepdims=True)
        normed = v * lax.rsqrt(mean + 1e-05) * gain[0]
        for t in range(steps):
            rows_out[t, pl.ds(r, 1), pl.ds(pl.multiple_of(g * width, 128), width)] = normed[
                t : t + 1
            ]
        update = lax.dot_general(
            left[0], right[0, 0], (((0,), (0,)), ((), ())), preferred_element_type=F32
        )
        for h in range(per_group):
            span = slice(h * head_size, (h + 1) * head_size)
            final[0, h] = (
                keep[0, h : h + 1] * s0[span].astype(F32) + update[span]
            ).astype(BF16)

    @pl.when(arrived)
    def _():
        run(came[...])

    @pl.when(jnp.logical_not(arrived))
    def _():
        run(resident[...])

    @pl.when((r == pl.num_programs(0) - 1) & (g == pl.num_programs(1) - 1))
    def _():
        out[...] = rows_out[...].astype(BF16)


def update_rows(flags, came, resident, scale, y0, gain, keep, left, right, reads):
    rows, heads, head_size, state_size = resident.shape
    groups = reads.shape[1]
    steps = scale.shape[1]
    per_group = heads // groups
    width = per_group * head_size
    pieces, _, piece_heads = came.shape[:3]
    wide = lambda lines: pl.BlockSpec((1, lines, width), lambda r, g, f: (r, 0, g))
    small = pl.BlockSpec((1, 1, 4 * steps, state_size), lambda r, g, f: (r, g, 0, 0))
    state_spec = pl.BlockSpec(
        (1, per_group, head_size, state_size), lambda r, g, f: (r, g, 0, 0)
    )
    return pl.pallas_call(
        functools.partial(update_kernel, steps),
        grid_spec=pltpu.PrefetchScalarGridSpec(
            num_scalar_prefetch=1,
            grid=(rows, groups),
            in_specs=[
                pl.BlockSpec(
                    (pieces // groups, 1, piece_heads, head_size, state_size),
                    lambda r, g, f: (g, r, 0, 0, 0),
                ),
                state_spec,
                wide(steps),
                wide(steps),
                wide(steps),
                pl.BlockSpec((1, per_group, state_size), lambda r, g, f: (r, g, 0)),
                wide(4 * steps),
                small,
                small,
            ],
            out_specs=[
                pl.BlockSpec((steps, rows, heads * head_size), lambda r, g, f: (0, 0, 0)),
                state_spec,
            ],
            scratch_shapes=[pltpu.VMEM((steps, rows, heads * head_size), F32)],
        ),
        out_shape=[
            jax.ShapeDtypeStruct((steps, rows, heads * head_size), BF16),
            jax.ShapeDtypeStruct(resident.shape, BF16),
        ],
        compiler_params=pltpu.CompilerParams(vmem_limit_bytes=40 * 1024 * 1024),
    )(flags, came, resident, scale, y0, gain, keep, left, right, reads)


def per_device(
    pre_state,
    pre_conv,
    resident_state,
    resident_conv,
    source_slot,
    target_row,
    conv_input,
    delta_raw,
    gate_input,
    active,
    conv_weight,
    conv_bias,
    delta_bias,
    decay_log,
    skip_gain,
    norm_gain,
):
    devices = lax.axis_size("rows")
    slots, heads, head_size, state_size = pre_state.shape
    rows = resident_state.shape[0]
    all_source = lax.all_gather(source_slot, "rows", axis=0, tiled=True)
    all_target = lax.all_gather(target_row, "rows", axis=0, tiled=True)
    matches = all_target[None, :] == jnp.arange(devices * rows, dtype=jnp.int32)[:, None]
    arrival = jnp.any(matches, axis=1)
    slot_for_row = jnp.sum(jnp.where(matches, all_source[None, :], 0), axis=1)
    first = lax.axis_index("rows") * rows
    own_arrival = lax.dynamic_slice_in_dim(arrival, first, rows)
    own_slot = lax.dynamic_slice_in_dim(slot_for_row, first, rows)

    piece_heads = heads // devices
    pieces = pre_state.reshape(slots, devices, piece_heads, head_size, state_size)
    held = lax.all_to_all(pieces, "rows", split_axis=1, concat_axis=0, tiled=True)
    held = held.reshape(devices * slots, piece_heads, head_size, state_size)
    outgoing = held[slot_for_row].reshape(devices, rows, piece_heads, head_size, state_size)
    came = lax.all_to_all(outgoing, "rows", split_axis=0, concat_axis=0, tiled=True)

    all_conv = lax.all_gather(pre_conv, "rows", axis=0, tiled=True)
    start_conv = jnp.where(own_arrival[:, None, None, None], all_conv[own_slot], resident_conv)
    final_conv, *small = prepare(
        start_conv,
        conv_input,
        delta_raw,
        gate_input,
        active,
        conv_weight,
        conv_bias,
        delta_bias,
        decay_log,
        skip_gain,
        norm_gain,
        state_size,
        head_size,
    )
    layer_output, final_state = update_rows(
        own_arrival.astype(jnp.int32), came, resident_state, *small
    )
    return layer_output, final_state, final_conv


def solution(mesh):
    in_specs = (
        P(("grp", "rows"), "heads", None, None),
        P(("grp", "rows"), None, "heads", None),
        P(("grp", "rows"), "heads", None, None),
        P(("grp", "rows"), None, "heads", None),
        P(("grp", "rows")),
        P(("grp", "rows")),
        P(None, ("grp", "rows"), "heads", None),
        P(None, ("grp", "rows"), "heads"),
        P(None, ("grp", "rows"), "heads"),
        P(None, ("grp", "rows")),
        P(None, "heads", None),
        P("heads", None),
        P("heads"),
        P("heads"),
        P("heads"),
        P("heads"),
    )
    out_specs = (
        P(None, ("grp", "rows"), "heads"),
        P(("grp", "rows"), "heads", None, None),
        P(("grp", "rows"), None, "heads", None),
    )
    return jax.shard_map(
        per_device, mesh=mesh, in_specs=in_specs, out_specs=out_specs, check_vma=False
    )
```

time: 244 us -> 201 us (0.82)
  other arithmetic: 45.6 us -> 4.28 us
  blocking collectives: 44.5 us -> 76.1 us
  local copies, waits for them, and re-layouts: 39.7 us -> 16.5 us
  starting transfers between devices: 21.8 us -> 12.1 us
  waiting for transfers between devices: 89.4 us -> 80 us
  Pallas kernels: 0 us -> 8.6 us
    all_gather x0 -> x1, blocking collectives: none -> 31.2 us  [per_device(): all_conv = lax.all_gather(pre_conv, 'rows', axis=0, tiled=True)]
    reduce_sum x4 -> x1, other arithmetic: 26.9 us -> 0.12 us  [prepare(): bc = jnp.sum(b[:, None] * c[:, :, None], axis=-1)]
    reshape x18 -> x3, local copies, waits for them, and re-layouts: 22 us -> 3.55 us  [the longest x1 3.22 us: per_device(): pre_state.reshape(slots, devices, piece_heads, head_size, state_size)]
    convert_element_type x6, other arithmetic: 16.2 us -> 0.45 us  [the longest x5 0.38 us: split_two(): return (high.astype(BF16), (values - high).astype(BF16))]
    all_to_all x4 -> x2, starting transfers between devices: 21.8 us -> 12.1 us  [the longest x1 7.38 us: per_device(): lax.all_to_all(pieces, 'rows', split_axis=1, concat_axis=0, tiled=True)]
    all_to_all x4 -> x2, waiting for transfers between devices: 89.4 us -> 80 us  [the longest x1 80 us: per_device(): lax.all_to_all(outgoing, 'rows', split_axis=0, concat_axis=0, tiled=True)]
    pallas_call x0 -> x1, Pallas kernels: none -> 8.6 us  [update_rows(): pl.pallas_call(functools.partial(update_kernel, steps), grid_spec=pltpu.P...]
    all_to_all x2 -> x0, local copies, waits for them, and re-layouts: 6.51 us -> none  [the longest x1 6.5 us: per_device(): lax.all_to_all(outgoing_state, 'rows', split_axis=0, concat_axis=2, tiled...]
  transfers between devices with their start and end apart: 4 -> 2, of which waited for: 2 -> 1; matrix products, arithmetic and copies ran while one was open for 11% -> 6% of each run, Pallas kernels for 0% -> 0%
where the time goes in v1:
time: 201 us; the launch traced here: 200 us
  waiting for transfers between devices  80 us (40%)
  blocking collectives  76.1 us (38%)
  local copies, waits for them, and re-layouts  16.5 us (8%)
  starting transfers between devices  12.1 us (6%)
  Pallas kernels  8.6 us (4%)
  other arithmetic  4.28 us (2%)
  between operations  2.61 us (1%)
    all_to_all x1, waiting for transfers between devices, per_device(): lax.all_to_all(outgoing, 'rows', split_axis=0, concat_axis=0, tiled=True)  80 us
    unnamed x1, blocking collectives  45 us
    all_gather x1, blocking collectives, per_device(): all_conv = lax.all_gather(pre_conv, 'rows', axis=0, tiled=True)  31.2 us
    pallas_call x1, Pallas kernels, update_rows(): pl.pallas_call(functools.partial(update_kernel, steps), grid_spec=pltpu.P...  8.6 us
    all_to_all x1, starting transfers between devices, per_device(): lax.all_to_all(pieces, 'rows', split_axis=1, concat_axis=0, tiled=True)  7.38 us
    unnamed x34, local copies, waits for them, and re-layouts  5.07 us
    all_to_all x1, starting transfers between devices, per_device(): lax.all_to_all(outgoing, 'rows', split_axis=0, concat_axis=0, tiled=True)  4.7 us
  transfers between devices with their start and end apart: 2, of which 1 were waited for; matrix products, arithmetic and copies ran while one was open for 6% of the time, Pallas kernels for 0%

profile of v1, /device:TPU:0, one launch (start us, length us, event | category | flops | bytes accessed | tf_op | source)
XLA Modules:
  0.0 200.1 jit_solution(2248798629918648040)
XLA Ops:
  0.7 3.2 %copy.128 = bf16[2,8,8,64,128]{4,3,2,0,1:T(8,128)(2,1)} copy(bf16[2,8,8,64,128]{4,3,2,1,0:T(8,128)(2,1)} %bitcast.533) | data formatting | bytes 4194304 | tf_op jit(solution)/shard_map/reshape | solution.py:219
  3.9 7.4 %all-to-all-start = ((bf16[2,8,8,64,128]{4,3,2,0,1:T(8,128)(2,1)}), bf16[2,8,8,64,128]{4,3,2,0,1:T(8,128)(2,1)S(1)}, u32[]{:S(2)}, u32[]{:S(2)}) async-start(bf16[2,8,8,64,128]{4,3,2,0,1:T(8,128)(2,1)} %copy.128), calls=%async_computation | async-start | bytes 4194304 | tf_op jit(solution)/shard_map/all_to_all | solution.py:220
  12.7 0.6 dynamic-slice
  13.3 0.8 dynamic-update-slice
  14.0 0.8 dynamic-update-slice.1
  14.8 45.0 %all-reduce.2 = (s32[8]{0:T(128)S(1)}, s32[8]{0:T(128)S(1)}) all-reduce(s32[8]{0:T(128)S(1)} %dynamic-update-slice, s32[8]{0:T(128)S(1)} %dynamic-update-slice.1), channel_id=1, replica_groups=mesh['grp'=2,'rows'=8,'heads'=2] {'rows'}, use_global_device_ids=true, to_apply=%add | all-reduce | flops 16 | bytes 128
  60.1 31.2 %all_gather.11 = bf16[16,3,2,2304]{3,2,1,0:T(2,128)(2,1)S(1)} all-gather(bf16[2,3,2,2304]{3,2,1,0:T(2,128)(2,1)S(1)} %copy-done.6), channel_id=1, replica_groups=mesh['grp'=2,'rows'=8,'heads'=2] {'rows'}, dimensions={0}, use_global_device_ids=true | all-gather | bytes 497664 | tf_op jit(solution)/shard_map/all_gather | solution.py:225
  91.4 0.8 gather_fusion.1
  92.2 0.2 broadcast_select_fusion
  92.7 0.3 fusion.35
  93.0 0.2 select_convert_fusion
  93.2 0.2 pad_maximum_fusion
  93.3 0.7 copy.156
  94.1 0.4 divide_multiply_fusion.3
  94.8 3.1 %gather_fusion = bf16[32,8,64,128]{3,2,1,0:T(8,128)(2,1)} fusion(bf16[16,8,64,128]{3,2,1,0:T(8,128)(2,1)S(1)} %bitcast.531, s32[1024]{0:T(1024)S(1)} %pad_clamp_fusion.1), kind=kCustom, calls=%fused_computation | custom fusion | bytes 8388736 | tf_op jit(solution)/shard_map/gather | solution.py:222
  97.9 4.7 %all-to-all-start.1 = ((bf16[8,4,8,64,128]{4,3,2,1,0:T(8,128)(2,1)}), bf16[8,4,8,64,128]{4,3,2,1,0:T(8,128)(2,1)}, u32[]{:S(2)}, u32[]{:S(2)}) async-start(bf16[8,4,8,64,128]{4,3,2,1,0:T(8,128)(2,1)} %bitcast.532), calls=%async_computation.1 | async-start | bytes 8388608 | tf_op jit(solution)/shard_map/all_to_all | solution.py:223
  102.6 0.5 divide_multiply_fusion.2
  103.6 0.2 copy.138
  104.3 0.1 mul.623
  104.9 0.1 mul.597
  105.1 0.1 mul.643
  106.7 0.2 mul.649
  106.9 0.2 mul.650
  107.1 0.2 broadcast_in_dim.179
  107.3 0.2 reshape.1193
  107.7 0.3 reduce-precision_convert_fusion
  108.1 0.2 maximum_maximum_fusion.left
  108.3 0.5 multiply_add_fusion.1
  108.9 0.4 maximum_multiply_fusion
  109.3 80.0 %all-to-all-done.1.came = bf16[8,4,8,64,128]{4,3,2,1,0:T(8,128)(2,1)} async-done(((bf16[8,4,8,64,128]{4,3,2,1,0:T(8,128)(2,1)}), bf16[8,4,8,64,128]{4,3,2,1,0:T(8,128)(2,1)}, u32[]{:S(2)}, u32[]{:S(2)}) %all-to-all-start.1) | async-done | bytes 4194336 | tf_op jit(solution)/shard_map/all_to_all | solution.py:223
  189.3 2.2 %copy-done = bf16[4,64,64,128]{3,2,1,0:T(8,128)(2,1)S(1)} copy-done((bf16[4,64,64,128]{3,2,1,0:T(8,128)(2,1)S(1)}, bf16[4,64,64,128]{3,2,1,0:T(8,128)(2,1)}, u32[]{:S(2)}) %copy-start) | copy-done | bytes 4194328
  191.5 8.6 %shard_map.175 = (bf16[4,4,4096]{2,1,0:T(4,128)(2,1)}, bf16[4,64,64,128]{3,2,1,0:T(8,128)(2,1)}) custom-call(s32[4]{0:T(128)S(1)} %get-tuple-element.40.flags, bf16[8,4,8,64,128]{4,3,2,1,0:T(8,128)(2,1)} %all-to-all-done.1.came, bf16[4,64,64,128]{3,2,1,0:T(8,128)(2,1)S(1)} %copy-done, f32[4,4,4096]{2,1,0:T(4,128)S(1)} %get-tuple-element.53.scale, ...), custom_call_target="tpu_custom_call" | custom-call | tf_op jit(solution)/shard_map/pallas_call | solution.py:155
  (97 shorter events, 4.0 us)
Async XLA Ops:
  0.6 10.7 %copy-start.9 = (s32[4,4]{1,0:T(4,128)S(1)}, s32[4,4]{1,0:T(4,128)}, u32[]{:S(2)}) copy-start(s32[4,4]{1,0:T(4,128)} %param.25) | copy-start | bytes 196
  0.6 12.0 %copy-start.12 = (f32[64]{0:T(128)S(1)}, f32[64]{0:T(128)}, u32[]{:S(2)}) copy-start(f32[64]{0:T(128)} %param.29) | copy-start | bytes 772
  0.7 12.0 %copy-start.13 = (u32[32]{0:T(128)S(1)}, u32[32]{0:T(128)}, u32[]{:S(2)}) copy-start(u32[32]{0:T(128)} %constant.52) | copy-start | bytes 388
  0.7 59.4 %copy-start.6 = (bf16[2,3,2,2304]{3,2,1,0:T(2,128)(2,1)S(1)}, bf16[2,3,2,2304]{3,2,1,0:T(2,128)(2,1)}, u32[]{:S(2)}) copy-start(bf16[2,3,2,2304]{3,2,1,0:T(2,128)(2,1)} %param.17) | copy-start | bytes 165892
  0.7 90.6 %copy-start.7 = (bf16[4,4,64]{2,1,0:T(4,128)(2,1)S(1)}, bf16[4,4,64]{2,1,0:T(4,128)(2,1)}, u32[]{:S(2)}) copy-start(bf16[4,4,64]{2,1,0:T(4,128)(2,1)} %param.23) | copy-start | bytes 6148
  0.7 90.6 %copy-start.10 = (f32[64]{0:T(128)S(1)}, f32[64]{0:T(128)}, u32[]{:S(2)}) copy-start(f32[64]{0:T(128)} %param.28) | copy-start | bytes 772
  0.7 91.5 %copy-start.3 = (bf16[4,3,2,2304]{3,2,1,0:T(2,128)(2,1)S(1)}, bf16[4,3,2,2304]{3,2,1,0:T(2,128)(2,1)}, u32[]{:S(2)}) copy-start(bf16[4,3,2,2304]{3,2,1,0:T(2,128)(2,1)} %param.19) | copy-start | bytes 331780
  0.7 92.0 %copy-start.1 = (bf16[4,4,2,2304]{3,2,1,0:T(2,128)(2,1)S(1)}, bf16[4,4,2,2304]{3,2,1,0:T(2,128)(2,1)}, u32[]{:S(2)}) copy-start(bf16[4,4,2,2304]{3,2,1,0:T(2,128)(2,1)} %param.22) | copy-start | bytes 442372
  3.9 90.1 %copy-start.5 = (f32[4,2,2304]{2,1,0:T(2,128)S(1)}, f32[4,2,2304]{2,1,0:T(2,128)}, u32[]{:S(2)}) copy-start(f32[4,2,2304]{2,1,0:T(2,128)} %param.26) | copy-start | bytes 221188
  3.9 90.1 %copy-start.4 = (f32[2,2304]{1,0:T(2,128)S(1)}, f32[2,2304]{1,0:T(2,128)}, u32[]{:S(2)}) copy-start(f32[2,2304]{1,0:T(2,128)} %param.27) | copy-start | bytes 55300
  3.9 90.9 %all-to-all-start = ((bf16[2,8,8,64,128]{4,3,2,0,1:T(8,128)(2,1)}), bf16[2,8,8,64,128]{4,3,2,0,1:T(8,128)(2,1)S(1)}, u32[]{:S(2)}, u32[]{:S(2)}) async-start(bf16[2,8,8,64,128]{4,3,2,0,1:T(8,128)(2,1)} %copy.128), calls=%async_computation | async-start | bytes 4194304 | tf_op jit(solution)/shard_map/all_to_all | solution.py:220
  97.9 6.8 %copy-start.11 = (f32[64]{0:T(128)S(1)}, f32[64]{0:T(128)}, u32[]{:S(2)}) copy-start(f32[64]{0:T(128)} %param.30) | copy-start | bytes 772
  97.9 91.3 %all-to-all-start.1 = ((bf16[8,4,8,64,128]{4,3,2,1,0:T(8,128)(2,1)}), bf16[8,4,8,64,128]{4,3,2,1,0:T(8,128)(2,1)}, u32[]{:S(2)}, u32[]{:S(2)}) async-start(bf16[8,4,8,64,128]{4,3,2,1,0:T(8,128)(2,1)} %bitcast.532), calls=%async_computation.1 | async-start | bytes 8388608 | tf_op jit(solution)/shard_map/all_to_all | solution.py:223
  102.6 5.0 %copy-start.8 = (f32[4096]{0:T(1024)S(1)}, f32[4096]{0:T(1024)}, u32[]{:S(2)}) copy-start(f32[4096]{0:T(1024)} %param.31) | copy-start | bytes 49156
  104.8 4.1 %copy-start.2 = (bf16[4,4,4096]{2,1,0:T(4,128)(2,1)S(1)}, bf16[4,4,4096]{2,1,0:T(4,128)(2,1)}, u32[]{:S(2)}) copy-start(bf16[4,4,4096]{2,1,0:T(4,128)(2,1)} %param.24) | copy-start | bytes 393220
  189.3 2.2 %copy-start = (bf16[4,64,64,128]{3,2,1,0:T(8,128)(2,1)S(1)}, bf16[4,64,64,128]{3,2,1,0:T(8,128)(2,1)}, u32[]{:S(2)}) copy-start(bf16[4,64,64,128]{3,2,1,0:T(8,128)(2,1)} %resident.1) | copy-start | bytes 12582916

commit v2 on v1

--- a/solution.py
+++ b/solution.py
@@ -185,6 +185,215 @@
     )(flags, came, resident, scale, y0, gain, keep, left, right, reads)
 
 
+def route_kernel(
+    inner, slots, rows, pre, pre_conv, info, came, came_conv, infos,
+    held, held_conv, out, out_conv, table,
+    local_sem, spread_send, spread_recv, line_send, line_recv, hop_send, hop_recv,
+    *buffers,
+):
+    devices = lax.axis_size("rows")
+    outer = devices // inner
+    half = len(buffers) // 2
+    lines = list(zip(buffers[:half], buffers[half:]))
+    prompts = buffers[0].shape[0]
+    me = lax.axis_index("rows")
+    z = me // inner
+    x = me % inner
+
+    barrier = pltpu.get_barrier_semaphore()
+    for j in range(1, devices):
+        pl.semaphore_signal(
+            barrier, inc=1, device_id={"rows": lax.rem(me + j, devices)},
+            device_id_type=pl.DeviceIdType.MESH,
+        )
+    pl.semaphore_wait(barrier, devices - 1)
+
+    def remote(src, dst, send, recv, peer):
+        return pltpu.make_async_remote_copy(
+            src_ref=src, dst_ref=dst, send_sem=send, recv_sem=recv,
+            device_id={"rows": peer}, device_id_type=pl.DeviceIdType.MESH,
+        )
+
+    mine = pl.ds(me * slots, slots)
+    spread = []
+    for j in range(1, devices):
+        peer = lax.rem(me + j, devices)
+        for k, (src, dst) in enumerate((
+            (info.at[0], infos.at[me]),
+            (pre_conv.at[:, peer], held_conv.at[mine]),
+            (pre.at[:, peer], held.at[mine]),
+        )):
+            spread.append(remote(src, dst, spread_send.at[k, j], spread_recv.at[k, j], peer))
+    for copy in spread:
+        copy.start()
+    own = [
+        pltpu.make_async_copy(info.at[0], infos.at[me], local_sem.at[0]),
+        pltpu.make_async_copy(pre_conv.at[:, me], held_conv.at[mine], local_sem.at[1]),
+        pltpu.make_async_copy(pre.at[:, me], held.at[mine], local_sem.at[2]),
+    ]
+    for copy in own:
+        copy.start()
+    for copy in own:
+        copy.wait()
+    for copy in spread:
+        copy.wait_recv()
+    to_table = pltpu.make_async_copy(infos, table, local_sem.at[3])
+    to_table.start()
+    to_table.wait()
+
+    def pick(q, carry):
+        slot = table[q, 0, 0]
+        lines[0][0][q] = held[slot]
+        lines[0][1][q] = held_conv[slot]
+        return carry
+
+    lax.fori_loop(0, prompts, pick, 0)
+
+    def prompt_of(row):
+        def look(q, found):
+            return jnp.where(table[q, 0, 1] == row, q, found)
+
+        return lax.fori_loop(0, prompts, look, 0)
+
+    wanted = [
+        [prompt_of((z * inner + lax.rem(x + j, inner)) * rows + k) for k in range(rows)]
+        for j in range(inner)
+    ]
+
+    def hop(block, j):
+        peer = z * inner + lax.rem(x + j, inner)
+        piece = block * inner + x
+        return [
+            remote(out.at[block, j - 1], came.at[piece], hop_send.at[0, block, j - 1],
+                   hop_recv.at[0, block, j - 1], peer),
+            remote(out_conv.at[block, j - 1], came_conv.at[piece], hop_send.at[1, block, j - 1],
+                   hop_recv.at[1, block, j - 1], peer),
+        ]
+
+    def deliver(block, line, line_conv):
+        for j in range(1, inner):
+            for k in range(rows):
+                out[block, j - 1, k] = line[wanted[j][k]]
+                out_conv[block, j - 1, k] = line_conv[wanted[j][k]]
+            for copy in hop(block, j):
+                copy.start()
+        for k in range(rows):
+            came[block * inner + x, k] = line[wanted[0][k]]
+            came_conv[block * inner + x, k] = line_conv[wanted[0][k]]
+
+    def landed(s, way):
+        return lines[0] if s < 0 else lines[1 + (way + 1) // 2 * (outer - 1) + s]
+
+    def step_copies(s, way):
+        side = (way + 1) // 2
+        return [
+            remote(src, dst, line_send.at[k, side, s], line_recv.at[k, side, s], me + way * inner)
+            for k, (src, dst) in enumerate(zip(landed(s - 1, way), landed(s, way)))
+        ]
+
+    def sends(s, way):
+        ok = (z - way * s >= 0) & (z - way * s < outer) & (z + way >= 0) & (z + way < outer)
+        return ok
+
+    def receives(s, way):
+        origin = z - way - way * s
+        return (origin >= 0) & (origin < outer)
+
+    def arrivals(s, way):
+        side = (way + 1) // 2
+        return [
+            remote(dst, dst, line_send.at[k, side, s], line_recv.at[k, side, s], me - way * inner)
+            for k, dst in enumerate(landed(s, way))
+        ]
+
+    for s in range(outer - 1):
+        for way in (1, -1):
+            @pl.when(sends(s, way))
+            def _():
+                for copy in step_copies(s, way):
+                    copy.start()
+
+        if s == 0:
+            deliver(z, *lines[0])
+        else:
+            for way in (1, -1):
+                @pl.when(receives(s - 1, way))
+                def _():
+                    deliver(z - way * s, *landed(s - 1, way))
+
+        for way in (1, -1):
+            @pl.when(receives(s, way))
+            def _():
+                for copy in arrivals(s, way):
+                    copy.wait_recv()
+
+    for way in (1, -1):
+        @pl.when(receives(outer - 2, way))
+        def _():
+            deliver(z - way * (outer - 1), *landed(outer - 2, way))
+
+    for copy in spread:
+        copy.wait_send()
+    for s in range(outer - 1):
+        for way in (1, -1):
+            @pl.when(sends(s, way))
+            def _():
+                for copy in step_copies(s, way):
+                    copy.wait_send()
+
+    for block in range(outer):
+        for j in range(1, inner):
+            source = lax.rem(x + inner - j, inner)
+            piece = block * inner + source
+            for copy in hop(block, j):
+                copy.wait_send()
+            remote(out.at[block, j - 1], came.at[piece], hop_send.at[0, block, j - 1],
+                   hop_recv.at[0, block, j - 1], z * inner + source).wait_recv()
+            remote(out_conv.at[block, j - 1], came_conv.at[piece], hop_send.at[1, block, j - 1],
+                   hop_recv.at[1, block, j - 1], z * inner + source).wait_recv()
+
+
+def route(pre, pre_conv, info, rows):
+    slots, devices, piece_heads, head_size, state_size = pre.shape
+    lines = pre_conv.shape[2]
+    inner = 4 if devices % 16 == 0 else 2
+    outer = devices // inner
+    prompts = devices
+    state = (piece_heads, head_size, state_size)
+    conv = (lines, 128)
+    vmem = pl.BlockSpec(memory_space=pltpu.VMEM)
+    dma = pltpu.SemaphoreType.DMA
+    return pl.pallas_call(
+        functools.partial(route_kernel, inner, slots, rows),
+        in_specs=[pl.BlockSpec(memory_space=pl.ANY), vmem, vmem],
+        out_specs=[vmem, vmem, vmem],
+        out_shape=[
+            jax.ShapeDtypeStruct((devices, rows) + state, BF16),
+            jax.ShapeDtypeStruct((devices, rows) + conv, BF16),
+            jax.ShapeDtypeStruct((devices, 1, 128), jnp.int32),
+        ],
+        scratch_shapes=[
+            pltpu.VMEM((devices * slots,) + state, BF16),
+            pltpu.VMEM((devices * slots,) + conv, BF16),
+            pltpu.VMEM((outer, inner - 1, rows) + state, BF16),
+            pltpu.VMEM((outer, inner - 1, rows) + conv, BF16),
+            pltpu.SMEM((devices, 1, 128), jnp.int32),
+            dma((4,)),
+            dma((3, devices)),
+            dma((3, devices)),
+            dma((2, 2, outer - 1)),
+            dma((2, 2, outer - 1)),
+            dma((2, outer, inner - 1)),
+            dma((2, outer, inner - 1)),
+        ]
+        + [pltpu.VMEM((prompts,) + state, BF16)] * (2 * outer - 1)
+        + [pltpu.VMEM((prompts,) + conv, BF16)] * (2 * outer - 1),
+        compiler_params=pltpu.CompilerParams(
+            collective_id=0, has_side_effects=True, vmem_limit_bytes=56 * 1024 * 1024
+        ),
+    )(pre, pre_conv, info)
+
+
 def per_device(
     pre_state,
     pre_conv,
@@ -206,24 +415,21 @@
     devices = lax.axis_size("rows")
     slots, heads, head_size, state_size = pre_state.shape
     rows = resident_state.shape[0]
-    all_source = lax.all_gather(source_slot, "rows", axis=0, tiled=True)
-    all_target = lax.all_gather(target_row, "rows", axis=0, tiled=True)
-    matches = all_target[None, :] == jnp.arange(devices * rows, dtype=jnp.int32)[:, None]
-    arrival = jnp.any(matches, axis=1)
-    slot_for_row = jnp.sum(jnp.where(matches, all_source[None, :], 0), axis=1)
-    first = lax.axis_index("rows") * rows
-    own_arrival = lax.dynamic_slice_in_dim(arrival, first, rows)
-    own_slot = lax.dynamic_slice_in_dim(slot_for_row, first, rows)
-
     piece_heads = heads // devices
     pieces = pre_state.reshape(slots, devices, piece_heads, head_size, state_size)
-    held = lax.all_to_all(pieces, "rows", split_axis=1, concat_axis=0, tiled=True)
-    held = held.reshape(devices * slots, piece_heads, head_size, state_size)
-    outgoing = held[slot_for_row].reshape(devices, rows, piece_heads, head_size, state_size)
-    came = lax.all_to_all(outgoing, "rows", split_axis=0, concat_axis=0, tiled=True)
-
-    all_conv = lax.all_gather(pre_conv, "rows", axis=0, tiled=True)
-    start_conv = jnp.where(own_arrival[:, None, None, None], all_conv[own_slot], resident_conv)
+    conv_size = pre_conv[0].size // devices
+    lines = -(-conv_size // (16 * 128)) * 16
+    conv_pieces = jnp.pad(
+        pre_conv.reshape(slots, devices, conv_size), ((0, 0), (0, 0), (0, lines * 128 - conv_size))
+    ).reshape(slots, devices, lines, 128)
+    info = jnp.pad(jnp.stack([source_slot, target_row], axis=1), ((0, 0), (0, 126)))
+    came, came_conv, infos = route(pieces, conv_pieces, info.reshape(1, 1, 128), rows)
+
+    own_rows = lax.axis_index("rows") * rows + jnp.arange(rows, dtype=jnp.int32)
+    own_arrival = jnp.any(infos[:, 0, 1][None, :] == own_rows[:, None], axis=1)
+    arrived_conv = came_conv.reshape(devices, rows, lines * 128)[..., :conv_size]
+    arrived_conv = arrived_conv.swapaxes(0, 1).reshape(resident_conv.shape)
+    start_conv = jnp.where(own_arrival[:, None, None, None], arrived_conv, resident_conv)
     final_conv, *small = prepare(
         start_conv,
         conv_input,

time: 201 us -> 174 us (0.87)
  Pallas kernels: 8.6 us -> 148 us
  waiting for transfers between devices: 80 us -> 0 us
  blocking collectives: 76.1 us -> 0 us
  starting transfers between devices: 12.1 us -> 0 us
  other arithmetic: 4.28 us -> 7.69 us
    pallas_call x0 -> x1, Pallas kernels: none -> 142 us  [route(): pl.pallas_call(functools.partial(route_kernel, inner, slots, rows), in_sp...]
    all_to_all x2 -> x0, waiting for transfers between devices: 80 us -> none  [the longest x1 80 us: per_device(): lax.all_to_all(outgoing, 'rows', split_axis=0, concat_axis=0, tiled=True)]
    unnamed x1 -> x0, blocking collectives: 45 us -> none
    all_gather x1 -> x0, blocking collectives: 31.2 us -> none  [per_device(): all_conv = lax.all_gather(pre_conv, 'rows', axis=0, tiled=True)]
    all_to_all x2 -> x0, starting transfers between devices: 12.1 us -> none  [the longest x1 7.38 us: per_device(): lax.all_to_all(pieces, 'rows', split_axis=1, concat_axis=0, tiled=True)]
    gather x2 -> x0, local copies, waits for them, and re-layouts: 3.87 us -> none  [the longest x1 3.1 us: per_device(): held[slot_for_row]]
    pallas_call x1, Pallas kernels: 8.6 us -> 6.3 us  [update_rows(): pl.pallas_call(functools.partial(update_kernel, steps), grid_spec=pltpu.P...]
    unnamed x34 -> x22, local copies, waits for them, and re-layouts: 5.07 us -> 5.8 us
  transfers between devices with their start and end apart: 2 -> 0, of which waited for: 1 -> 0; matrix products, arithmetic and copies ran while one was open for 6% -> 0% of each run, Pallas kernels for 0% -> 0%
where the time goes in v2:
time: 174 us; the launch traced here: 173 us
  Pallas kernels  148 us (85%)
  local copies, waits for them, and re-layouts  14.5 us (8%)
  other arithmetic  7.69 us (4%)
  between operations  2.59 us (1%)
    pallas_call x1, Pallas kernels, route(): pl.pallas_call(functools.partial(route_kernel, inner, slots, rows), in_sp...  142 us
    pallas_call x1, Pallas kernels, update_rows(): pl.pallas_call(functools.partial(update_kernel, steps), grid_spec=pltpu.P...  6.3 us
    unnamed x22, local copies, waits for them, and re-layouts  5.8 us

profile of v2, /device:TPU:0, one launch (start us, length us, event | category | flops | bytes accessed | tf_op | source)
XLA Modules:
  0.0 173.1 jit_solution(6294803603111220967)
XLA Ops:
  2.1 0.5 pad_bitcast_fusion.1.info
  2.6 0.7 exponential_negate_fusion
  3.3 0.7 fusion.117
  4.1 0.7 broadcast_compare_fusion
  4.9 0.8 fusion.116
  5.8 0.9 reshape.1189
  6.8 0.6 copy.114
  7.4 0.8 slice_bitcast_fusion.3
  8.2 0.8 broadcast_select_fusion.1.gain
  9.0 0.2 mul.649
  9.2 0.2 mul.650
  9.5 0.2 broadcast_in_dim.159
  9.7 0.2 reshape.1192
  9.9 142.0 %shard_map.175 = (bf16[8,4,8,64,128]{4,3,2,1,0:T(8,128)(2,1)}, bf16[8,4,16,128]{3,2,1,0:T(8,128)(2,1)}, s32[8,1,128]{2,1,0:T(1,128)}) custom-call(bf16[2,8,8,64,128]{4,3,2,1,0:T(8,128)(2,1)} %bitcast.538, bf16[2,8,16,128]{3,2,1,0:T(8,128)(2,1)} %copy.114, s32[1,1,128]{2,1,0:T(1,128)} %pad_bitcast_fusion.1.info), custom_call_target="tpu_custom_call" | custom-call | tf_op jit(solution)/shard_map/pallas_call | solution.py:366
  151.9 1.0 slice_reduce_fusion
  152.9 0.2 compare_reduce_fusion
  153.1 0.9 reshape.1193
  154.2 0.2 reshape.1194
  154.4 0.2 broadcast_select_fusion
  154.6 0.3 fusion.35
  154.9 0.2 select_convert_fusion
  155.2 0.7 copy.101
  156.0 0.4 divide_multiply_fusion.3
  156.4 0.4 divide_multiply_fusion.2
  157.4 0.3 reduce-precision_convert_fusion
  158.0 0.2 copy.83
  161.2 0.5 multiply_add_fusion.1
  161.8 0.4 maximum_multiply_fusion
  162.2 0.2 maximum_maximum_fusion.left
  162.4 2.2 %copy-done = bf16[4,64,64,128]{3,2,1,0:T(8,128)(2,1)S(1)} copy-done((bf16[4,64,64,128]{3,2,1,0:T(8,128)(2,1)S(1)}, bf16[4,64,64,128]{3,2,1,0:T(8,128)(2,1)}, u32[]{:S(2)}) %copy-start) | copy-done | bytes 4194328
  164.6 2.2 %copy-done.1 = bf16[8,4,8,64,128]{4,3,2,1,0:T(8,128)(2,1)S(1)} copy-done((bf16[8,4,8,64,128]{4,3,2,1,0:T(8,128)(2,1)S(1)}, bf16[8,4,8,64,128]{4,3,2,1,0:T(8,128)(2,1)}, u32[]{:S(2)}) %copy-start.1) | copy-done | bytes 4194328
  166.8 6.3 %shard_map.176 = (bf16[4,4,4096]{2,1,0:T(4,128)(2,1)}, bf16[4,64,64,128]{3,2,1,0:T(8,128)(2,1)}) custom-call(s32[4]{0:T(128)S(1)} %convert_element_type.263.flags, bf16[8,4,8,64,128]{4,3,2,1,0:T(8,128)(2,1)S(1)} %copy-done.1, bf16[4,64,64,128]{3,2,1,0:T(8,128)(2,1)S(1)} %copy-done, f32[4,4,4096]{2,1,0:T(4,128)S(1)} %get-tuple-element.49.scale, ...), custom_call_target="tpu_custom_call" | custom-call | tf_op jit(solution)/shard_map/pallas_call | solution.py:155
  (80 shorter events, 4.2 us)
Async XLA Ops:
  0.6 153.9 %copy-start.2 = (bf16[4,4,2,2304]{3,2,1,0:T(2,128)(2,1)S(1)}, bf16[4,4,2,2304]{3,2,1,0:T(2,128)(2,1)}, u32[]{:S(2)}) copy-start(bf16[4,4,2,2304]{3,2,1,0:T(2,128)(2,1)} %param.22) | copy-start | bytes 442372
  0.6 155.3 %copy-start.5 = (f32[2,2304]{1,0:T(2,128)S(1)}, f32[2,2304]{1,0:T(2,128)}, u32[]{:S(2)}) copy-start(f32[2,2304]{1,0:T(2,128)} %param.27) | copy-start | bytes 55300
  0.7 153.7 %copy-start.4 = (bf16[4,3,2,2304]{3,2,1,0:T(2,128)(2,1)S(1)}, bf16[4,3,2,2304]{3,2,1,0:T(2,128)(2,1)}, u32[]{:S(2)}) copy-start(bf16[4,3,2,2304]{3,2,1,0:T(2,128)(2,1)} %param.19) | copy-start | bytes 331780
  9.7 149.0 %copy-start.6 = (bf16[4,4,64]{2,1,0:T(4,128)(2,1)S(1)}, bf16[4,4,64]{2,1,0:T(4,128)(2,1)}, u32[]{:S(2)}) copy-start(bf16[4,4,64]{2,1,0:T(4,128)(2,1)} %param.23) | copy-start | bytes 6148
  9.7 148.9 %copy-start.7 = (f32[64]{0:T(128)S(1)}, f32[64]{0:T(128)}, u32[]{:S(2)}) copy-start(f32[64]{0:T(128)} %param.28) | copy-start | bytes 772
  9.9 148.8 %copy-start.8 = (f32[64]{0:T(128)S(1)}, f32[64]{0:T(128)}, u32[]{:S(2)}) copy-start(f32[64]{0:T(128)} %param.30) | copy-start | bytes 772
  155.2 6.5 %copy-start.3 = (bf16[4,4,4096]{2,1,0:T(4,128)(2,1)S(1)}, bf16[4,4,4096]{2,1,0:T(4,128)(2,1)}, u32[]{:S(2)}) copy-start(bf16[4,4,4096]{2,1,0:T(4,128)(2,1)} %param.24) | copy-start | bytes 393220
  162.4 2.2 %copy-start = (bf16[4,64,64,128]{3,2,1,0:T(8,128)(2,1)S(1)}, bf16[4,64,64,128]{3,2,1,0:T(8,128)(2,1)}, u32[]{:S(2)}) copy-start(bf16[4,64,64,128]{3,2,1,0:T(8,128)(2,1)} %resident.1) | copy-start | bytes 12582916
  164.6 2.2 %copy-start.1 = (bf16[8,4,8,64,128]{4,3,2,1,0:T(8,128)(2,1)S(1)}, bf16[8,4,8,64,128]{4,3,2,1,0:T(8,128)(2,1)}, u32[]{:S(2)}) copy-start(bf16[8,4,8,64,128]{4,3,2,1,0:T(8,128)(2,1)} %get-tuple-element.9.came) | copy-start | bytes 12582916

commit v3 on v1

--- a/solution.py
+++ b/solution.py
@@ -9,6 +9,7 @@
 
 F32 = jnp.float32
 BF16 = jnp.bfloat16
+CHUNKS = 2
 
 
 def split_two(values):
@@ -181,8 +182,249 @@
             jax.ShapeDtypeStruct((steps, rows, heads * head_size), BF16),
             jax.ShapeDtypeStruct(resident.shape, BF16),
         ],
-        compiler_params=pltpu.CompilerParams(vmem_limit_bytes=40 * 1024 * 1024),
+        compiler_params=pltpu.CompilerParams(vmem_limit_bytes=56 * 1024 * 1024),
     )(flags, came, resident, scale, y0, gain, keep, left, right, reads)
+
+
+def route_kernel(
+    inner, slots, rows, chunks, pre, pre_conv, info, came, came_conv, infos, table,
+    local_sem, spread_send, spread_recv, line_send, line_recv, hop_send, hop_recv,
+    *buffers,
+):
+    devices = lax.axis_size("rows")
+    outer = devices // inner
+    part = pre.shape[2] // chunks
+    count = 2 * outer + 1
+    state_bufs = [buffers[c * count : (c + 1) * count] for c in range(chunks)]
+    conv_bufs = buffers[chunks * count :]
+    prompts = conv_bufs[2].shape[0]
+    me = lax.axis_index("rows")
+    z = me // inner
+    x = me % inner
+    mine = pl.ds(me * slots, slots)
+
+    barrier = pltpu.get_barrier_semaphore()
+    for j in range(1, devices):
+        pl.semaphore_signal(
+            barrier, inc=1, device_id={"rows": lax.rem(me + j, devices)},
+            device_id_type=pl.DeviceIdType.MESH,
+        )
+    pl.semaphore_wait(barrier, devices - 1)
+
+    def remote(src, dst, send, recv, peer):
+        return pltpu.make_async_remote_copy(
+            src_ref=src, dst_ref=dst, send_sem=send, recv_sem=recv,
+            device_id={"rows": peer}, device_id_type=pl.DeviceIdType.MESH,
+        )
+
+    def heads_of(c):
+        return pl.ds(c * part, part)
+
+    def sets(c):
+        return [state_bufs[c]] + ([conv_bufs] if c == 0 else [])
+
+    def pairs(c, peer):
+        result = [(pre.at[:, peer, heads_of(c)], state_bufs[c][0].at[mine])]
+        if c == 0:
+            result.append((pre_conv.at[:, peer], conv_bufs[0].at[mine]))
+            result.append((info.at[0], infos.at[me]))
+        return result
+
+    def spread(c):
+        copies = []
+        for j in sorted(range(1, devices), key=lambda j: (abs(j - devices // 2), j)):
+            peer = lax.rem(me + j, devices)
+            for k, (src, dst) in reversed(list(enumerate(pairs(c, peer)))):
+                copies.append(
+                    remote(src, dst, spread_send.at[k, c, j], spread_recv.at[k, c, j], peer)
+                )
+        return copies
+
+    def keep(c):
+        return [
+            pltpu.make_async_copy(src, dst, local_sem.at[k, c])
+            for k, (src, dst) in enumerate(pairs(c, me))
+        ]
+
+    def start_spread(c):
+        for copy in spread(c) + keep(c):
+            copy.start()
+
+    start_spread(0)
+    for copy in keep(0):
+        copy.wait()
+    for copy in spread(0):
+        copy.wait_recv()
+    if chunks > 1:
+        start_spread(1)
+    to_table = pltpu.make_async_copy(infos, table, local_sem.at[3, 0])
+    to_table.start()
+    to_table.wait()
+
+    def prompt_of(row):
+        def look(q, found):
+            return jnp.where(table[q, 0, 1] == row, q, found)
+
+        return lax.fori_loop(0, prompts, look, 0)
+
+    wanted = [
+        [prompt_of((z * inner + lax.rem(x + j, inner)) * rows + k) for k in range(rows)]
+        for j in range(inner)
+    ]
+
+    def target(k, c, piece):
+        return came.at[piece, :, heads_of(c)] if k == 0 else came_conv.at[piece]
+
+    def hop(c, block, j, piece, peer):
+        return [
+            remote(bufs[1].at[block, j - 1], target(k, c, piece), hop_send.at[k, c, block, j - 1],
+                   hop_recv.at[k, c, block, j - 1], peer)
+            for k, bufs in enumerate(sets(c))
+        ]
+
+    def landed(s, way):
+        return 2 if s < 0 else 3 + (way + 1) // 2 * (outer - 1) + s
+
+    def deliver(c, block, s, way):
+        piece = block * inner + x
+        for j in range(1, inner):
+            for k in range(rows):
+                for bufs in sets(c):
+                    bufs[1][block, j - 1, k] = bufs[landed(s, way)][wanted[j][k]]
+            for copy in hop(c, block, j, piece, z * inner + lax.rem(x + j, inner)):
+                copy.start()
+        for k in range(rows):
+            came[piece, k, heads_of(c)] = state_bufs[c][landed(s, way)][wanted[0][k]]
+            if c == 0:
+                came_conv[piece, k] = conv_bufs[landed(s, way)][wanted[0][k]]
+
+    def step_copies(c, s, way):
+        side = (way + 1) // 2
+        return [
+            remote(bufs[landed(s - 1, way)], bufs[landed(s, way)], line_send.at[k, c, side, s],
+                   line_recv.at[k, c, side, s], me + way * inner)
+            for k, bufs in enumerate(sets(c))
+        ]
+
+    def arrivals(c, s, way):
+        side = (way + 1) // 2
+        return [
+            remote(bufs[landed(s, way)], bufs[landed(s, way)], line_send.at[k, c, side, s],
+                   line_recv.at[k, c, side, s], me - way * inner)
+            for k, bufs in enumerate(sets(c))
+        ]
+
+    def sends(s, way):
+        return (z - way * s >= 0) & (z - way * s < outer) & (z + way >= 0) & (z + way < outer)
+
+    def receives(s, way):
+        origin = z - way - way * s
+        return (origin >= 0) & (origin < outer)
+
+    for c in range(chunks):
+        if c > 0:
+            for copy in keep(c):
+                copy.wait()
+            for copy in spread(c):
+                copy.wait_recv()
+            if c + 1 < chunks:
+                start_spread(c + 1)
+
+        def pick(q, carry):
+            slot = table[q, 0, 0]
+            for bufs in sets(c):
+                bufs[2][q] = bufs[0][slot]
+            return carry
+
+        lax.fori_loop(0, prompts, pick, 0)
+
+        for s in range(outer - 1):
+            for way in (1, -1):
+                @pl.when(sends(s, way))
+                def _():
+                    for copy in step_copies(c, s, way):
+                        copy.start()
+
+            if s == 0:
+                deliver(c, z, -1, 1)
+            else:
+                for way in (1, -1):
+                    @pl.when(receives(s - 1, way))
+                    def _():
+                        deliver(c, z - way * s, s - 1, way)
+
+            for way in (1, -1):
+                @pl.when(receives(s, way))
+                def _():
+                    for copy in arrivals(c, s, way):
+                        copy.wait_recv()
+
+        for way in (1, -1):
+            @pl.when(receives(outer - 2, way))
+            def _():
+                deliver(c, z - way * (outer - 1), outer - 2, way)
+
+    for c in range(chunks):
+        for copy in spread(c):
+            copy.wait_send()
+        for s in range(outer - 1):
+            for way in (1, -1):
+                @pl.when(sends(s, way))
+                def _():
+                    for copy in step_copies(c, s, way):
+                        copy.wait_send()
+        for block in range(outer):
+            for j in range(1, inner):
+                source = lax.rem(x + inner - j, inner)
+                for copy in hop(c, block, j, block * inner + source, z * inner + source):
+                    copy.wait_send()
+                    copy.wait_recv()
+
+
+def route(pre, pre_conv, info, rows):
+    slots, devices, piece_heads, head_size, state_size = pre.shape
+    lines = pre_conv.shape[2]
+    inner = 4 if devices % 16 == 0 else 2
+    outer = devices // inner
+    prompts = devices
+    chunks = min(CHUNKS, piece_heads)
+    state = (piece_heads, head_size, state_size)
+    part = (piece_heads // chunks, head_size, state_size)
+
+    def buffers(item):
+        return [
+            pltpu.VMEM((devices * slots,) + item, BF16),
+            pltpu.VMEM((outer, inner - 1, rows) + item, BF16),
+        ] + [pltpu.VMEM((prompts,) + item, BF16)] * (2 * outer - 1)
+
+    conv = (lines, 128)
+    vmem = pl.BlockSpec(memory_space=pltpu.VMEM)
+    dma = pltpu.SemaphoreType.DMA
+    return pl.pallas_call(
+        functools.partial(route_kernel, inner, slots, rows, chunks),
+        in_specs=[pl.BlockSpec(memory_space=pl.ANY), vmem, vmem],
+        out_specs=[vmem, vmem, vmem],
+        out_shape=[
+            jax.ShapeDtypeStruct((devices, rows) + state, BF16),
+            jax.ShapeDtypeStruct((devices, rows) + conv, BF16),
+            jax.ShapeDtypeStruct((devices, 1, 128), jnp.int32),
+        ],
+        scratch_shapes=[
+            pltpu.SMEM((devices, 1, 128), jnp.int32),
+            dma((4, chunks)),
+            dma((3, chunks, devices)),
+            dma((3, chunks, devices)),
+            dma((2, chunks, 2, outer - 1)),
+            dma((2, chunks, 2, outer - 1)),
+            dma((2, chunks, outer, inner - 1)),
+            dma((2, chunks, outer, inner - 1)),
+        ]
+        + buffers(part) * chunks
+        + buffers(conv),
+        compiler_params=pltpu.CompilerParams(
+            collective_id=0, has_side_effects=True, vmem_limit_bytes=56 * 1024 * 1024
+        ),
+    )(pre, pre_conv, info)
 
 
 def per_device(
@@ -206,24 +448,21 @@
     devices = lax.axis_size("rows")
     slots, heads, head_size, state_size = pre_state.shape
     rows = resident_state.shape[0]
-    all_source = lax.all_gather(source_slot, "rows", axis=0, tiled=True)
-    all_target = lax.all_gather(target_row, "rows", axis=0, tiled=True)
-    matches = all_target[None, :] == jnp.arange(devices * rows, dtype=jnp.int32)[:, None]
-    arrival = jnp.any(matches, axis=1)
-    slot_for_row = jnp.sum(jnp.where(matches, all_source[None, :], 0), axis=1)
-    first = lax.axis_index("rows") * rows
-    own_arrival = lax.dynamic_slice_in_dim(arrival, first, rows)
-    own_slot = lax.dynamic_slice_in_dim(slot_for_row, first, rows)
-
     piece_heads = heads // devices
     pieces = pre_state.reshape(slots, devices, piece_heads, head_size, state_size)
-    held = lax.all_to_all(pieces, "rows", split_axis=1, concat_axis=0, tiled=True)
-    held = held.reshape(devices * slots, piece_heads, head_size, state_size)
-    outgoing = held[slot_for_row].reshape(devices, rows, piece_heads, head_size, state_size)
-    came = lax.all_to_all(outgoing, "rows", split_axis=0, concat_axis=0, tiled=True)
-
-    all_conv = lax.all_gather(pre_conv, "rows", axis=0, tiled=True)
-    start_conv = jnp.where(own_arrival[:, None, None, None], all_conv[own_slot], resident_conv)
+    conv_size = pre_conv[0].size // devices
+    lines = -(-conv_size // (16 * 128)) * 16
+    conv_pieces = jnp.pad(
+        pre_conv.reshape(slots, devices, conv_size), ((0, 0), (0, 0), (0, lines * 128 - conv_size))
+    ).reshape(slots, devices, lines, 128)
+    info = jnp.pad(jnp.stack([source_slot, target_row], axis=1), ((0, 0), (0, 126)))
+    came, came_conv, infos = route(pieces, conv_pieces, info.reshape(1, 1, 128), rows)
+
+    own_rows = lax.axis_index("rows") * rows + jnp.arange(rows, dtype=jnp.int32)
+    own_arrival = jnp.any(infos[:, 0, 1][None, :] == own_rows[:, None], axis=1)
+    arrived_conv = came_conv.reshape(devices, rows, lines * 128)[..., :conv_size]
+    arrived_conv = arrived_conv.swapaxes(0, 1).reshape(resident_conv.shape)
+    start_conv = jnp.where(own_arrival[:, None, None, None], arrived_conv, resident_conv)
     final_conv, *small = prepare(
         start_conv,
         conv_input,

time: 201 us -> 172 us (0.86)
  Pallas kernels: 8.6 us -> 146 us
  waiting for transfers between devices: 80 us -> 0 us
  blocking collectives: 76.1 us -> 0 us
  starting transfers between devices: 12.1 us -> 0 us
  other arithmetic: 4.28 us -> 11.2 us
  local copies, waits for them, and re-layouts: 16.5 us -> 11.4 us
    pallas_call x0 -> x1, Pallas kernels: none -> 136 us  [route(): pl.pallas_call(functools.partial(route_kernel, inner, slots, rows, chunks...]
    all_to_all x2 -> x0, waiting for transfers between devices: 80 us -> none  [the longest x1 80 us: per_device(): lax.all_to_all(outgoing, 'rows', split_axis=0, concat_axis=0, tiled=True)]
    unnamed x1 -> x0, blocking collectives: 45 us -> none
    all_gather x1 -> x0, blocking collectives: 31.2 us -> none  [per_device(): all_conv = lax.all_gather(pre_conv, 'rows', axis=0, tiled=True)]
    all_to_all x2 -> x0, starting transfers between devices: 12.1 us -> none  [the longest x1 7.38 us: per_device(): lax.all_to_all(pieces, 'rows', split_axis=1, concat_axis=0, tiled=True)]
    gather x2 -> x0, local copies, waits for them, and re-layouts: 3.87 us -> none  [the longest x1 3.1 us: per_device(): held[slot_for_row]]
    unnamed x34 -> x18, local copies, waits for them, and re-layouts: 5.07 us -> 1.42 us
  transfers between devices with their start and end apart: 2 -> 0, of which waited for: 1 -> 0; matrix products, arithmetic and copies ran while one was open for 6% -> 0% of each run, Pallas kernels for 0% -> 0%
where the time goes in v3:
time: 172 us; the launch traced here: 171 us
  Pallas kernels  146 us (85%)
  local copies, waits for them, and re-layouts  11.4 us (7%)
  other arithmetic  11.2 us (7%)
  between operations  2.55 us (1%)
    pallas_call x1, Pallas kernels, route(): pl.pallas_call(functools.partial(route_kernel, inner, slots, rows, chunks...  136 us
    pallas_call x1, Pallas kernels, update_rows(): pl.pallas_call(functools.partial(update_kernel, steps), grid_spec=pltpu.P...  9.85 us

profile of v3, /device:TPU:0, one launch (start us, length us, event | category | flops | bytes accessed | tf_op | source)
XLA Modules:
  0.0 171.1 jit_solution(8947250770004757062)
XLA Ops:
  2.1 0.5 pad_bitcast_fusion.1.info
  2.6 0.7 exponential_negate_fusion
  3.3 0.7 fusion.117
  4.1 0.7 broadcast_compare_fusion
  4.9 0.8 fusion.116
  5.8 0.9 reshape.1189
  6.8 0.6 copy.114
  7.4 0.8 slice_bitcast_fusion.3
  8.2 1.5 broadcast_select_fusion.1.gain
  9.8 0.2 mul.649
  10.0 0.2 mul.650
  10.2 0.2 broadcast_in_dim.159
  10.4 0.2 reshape.1192
  10.7 136.0 %shard_map.175 = (bf16[8,4,8,64,128]{4,3,2,1,0:T(8,128)(2,1)}, bf16[8,4,16,128]{3,2,1,0:T(8,128)(2,1)}, s32[8,1,128]{2,1,0:T(1,128)}) custom-call(bf16[2,8,8,64,128]{4,3,2,1,0:T(8,128)(2,1)} %bitcast.538, bf16[2,8,16,128]{3,2,1,0:T(8,128)(2,1)} %copy.114, s32[1,1,128]{2,1,0:T(1,128)} %pad_bitcast_fusion.1.info), custom_call_target="tpu_custom_call" | custom-call | tf_op jit(solution)/shard_map/pallas_call | solution.py:403
  146.7 1.0 slice_reduce_fusion
  147.9 0.5 convert_element_type.263.flags
  148.4 0.9 reshape.1193
  149.4 0.2 reshape.1194
  149.7 0.2 broadcast_select_fusion
  149.9 0.3 fusion.35
  150.5 0.7 copy.101
  151.3 0.4 divide_multiply_fusion.3
  151.7 0.5 divide_multiply_fusion.2
  152.7 0.3 reduce-precision_convert_fusion
  153.3 0.7 maximum_maximum_fusion.2.reads
  153.9 0.2 copy.83
  154.3 0.6 copy.100.right
  156.4 0.8 broadcast_in_dim.171.keep
  158.4 0.5 multiply_add_fusion.1
  158.9 1.2 maximum_multiply_fusion
  160.2 1.0 maximum_maximum_fusion.left
  161.2 9.9 %shard_map.176 = (bf16[4,4,4096]{2,1,0:T(4,128)(2,1)}, bf16[4,64,64,128]{3,2,1,0:T(8,128)(2,1)}) custom-call(s32[4]{0:T(128)} %convert_element_type.263.flags, bf16[8,4,8,64,128]{4,3,2,1,0:T(8,128)(2,1)} %get-tuple-element.9.came, bf16[4,64,64,128]{3,2,1,0:T(8,128)(2,1)} %resident.1, f32[4,4,4096]{2,1,0:T(4,128)} %get-tuple-element.49.scale, ...), custom_call_target="tpu_custom_call" | custom-call | tf_op jit(solution)/shard_map/pallas_call | solution.py:156
  (76 shorter events, 4.4 us)
Async XLA Ops:
  0.6 149.2 %copy-start = (bf16[4,4,2,2304]{3,2,1,0:T(2,128)(2,1)S(1)}, bf16[4,4,2,2304]{3,2,1,0:T(2,128)(2,1)}, u32[]{:S(2)}) copy-start(bf16[4,4,2,2304]{3,2,1,0:T(2,128)(2,1)} %param.22) | copy-start | bytes 442372
  0.6 150.6 %copy-start.3 = (f32[2,2304]{1,0:T(2,128)S(1)}, f32[2,2304]{1,0:T(2,128)}, u32[]{:S(2)}) copy-start(f32[2,2304]{1,0:T(2,128)} %param.27) | copy-start | bytes 55300
  0.7 149.0 %copy-start.2 = (bf16[4,3,2,2304]{3,2,1,0:T(2,128)(2,1)S(1)}, bf16[4,3,2,2304]{3,2,1,0:T(2,128)(2,1)}, u32[]{:S(2)}) copy-start(bf16[4,3,2,2304]{3,2,1,0:T(2,128)(2,1)} %param.19) | copy-start | bytes 331780
  10.4 144.7 %copy-start.4 = (bf16[4,4,64]{2,1,0:T(4,128)(2,1)S(1)}, bf16[4,4,64]{2,1,0:T(4,128)(2,1)}, u32[]{:S(2)}) copy-start(bf16[4,4,64]{2,1,0:T(4,128)(2,1)} %param.23) | copy-start | bytes 6148
  10.4 144.7 %copy-start.5 = (f32[64]{0:T(128)S(1)}, f32[64]{0:T(128)}, u32[]{:S(2)}) copy-start(f32[64]{0:T(128)} %param.28) | copy-start | bytes 772
  10.6 144.6 %copy-start.6 = (f32[64]{0:T(128)S(1)}, f32[64]{0:T(128)}, u32[]{:S(2)}) copy-start(f32[64]{0:T(128)} %param.30) | copy-start | bytes 772
  150.5 8.4 %copy-start.1 = (bf16[4,4,4096]{2,1,0:T(4,128)(2,1)S(1)}, bf16[4,4,4096]{2,1,0:T(4,128)(2,1)}, u32[]{:S(2)}) copy-start(bf16[4,4,4096]{2,1,0:T(4,128)(2,1)} %param.24) | copy-start | bytes 393220
